TPU v7x, 128 devices: a whole 4x4x4 slice. The times are simulated.
128 devices in a mesh: tp: 4 (over y), ep: 8 (over x, core), etp: 4 (over z).
Axes of the slice: x: 4, y: 4, z: 4, core: 2. Of those that a mesh axis runs over, the one named last changes fastest.
Arguments:
- queries: bfloat16 [4096, 6144], P(('ep', 'etp'), 'tp'), may hold values from -128 to 128
- keys: bfloat16 [4096, 1024], P(('ep', 'etp'), 'tp'), may hold values from -4.5 to 4.5
- values: bfloat16 [4096, 1024], P(('ep', 'etp'), 'tp'), may hold values from -6 to 6
- residual: bfloat16 [32, 4, 32, 6144], P(('ep', 'etp'), 'tp'), may hold values from -6 to 6
- norm_gain: float32 [6144], replicated, may hold values from 0.1 to 1.9
- out_weight: bfloat16 [6144, 6144], P('tp', 'etp'), may hold values from -0.078125 to 0.078125
- gate_weight: bfloat16 [8, 6144, 8192], P('ep', None, ('tp', 'etp')), may hold values from -0.078125 to 0.078125
- up_weight: bfloat16 [8, 6144, 8192], P('ep', None, ('tp', 'etp')), may hold values from -0.078125 to 0.078125
- down_weight: bfloat16 [8, 8192, 6144], P('ep', ('tp', 'etp')), may hold values from -0.0625 to 0.0625
- expert_ids: int32 [32, 4, 32, 2], P(('ep', 'etp'), 'tp'), may hold values from 0 to 7, all different within a row; in each aligned block of 32 rows (0 to 31, 32 to 63, ..., all dimensions but the last counted through in order) at most 10 rows name the same one
- route_weights: float32 [32, 4, 32, 2], P(('ep', 'etp'), 'tp'), may hold values from 0.1 to 1
Outputs:
- attention: bfloat16 [4096, 6144], P(('ep', 'etp'), 'tp')
- mixed: bfloat16 [32, 4, 32, 6144], P(('ep', 'etp'), 'tp')
Inputs may be any that keep to these rules, and one draw needn't show every extreme that they name: `expert_ids`: the 2 picks of a token differ; in each routing group of 32 tokens (the rows of one device) no expert is named by more than 10 tokens, a bound that some block reaches.
All inputs are finite; a program needn't handle non-finite values.
Results may differ from a plain program's by a relative error of at most 0.013.
Values may be sent and summed in bfloat16 or wider, within the bound.
No kernel may reach another device: no remote copies, remote signals or barrier semaphores. Data moves between devices by JAX's collectives and lax.ppermute only.
A program may use at most 192 MiB of HBM per device.

v0:
```python
import math

import jax
import jax.numpy as jnp
from jax import lax
from jax.sharding import PartitionSpec as P

HD = 128


def route_tables(ids, weights, experts, cap):
    tokens, top = ids.shape
    flat = ids.reshape(-1)
    hot = (flat[:, None] == jnp.arange(experts, dtype=jnp.int32)[None, :]).astype(jnp.int32)
    rank = jnp.cumsum(hot, axis=0) - hot
    slot = jnp.sum(rank * hot, axis=1).reshape(tokens, top)
    same_expert = ids[None, None, :, :] == jnp.arange(experts, dtype=jnp.int32)[:, None, None, None]
    same_slot = slot[None, None, :, :] == jnp.arange(cap, dtype=jnp.int32)[None, :, None, None]
    match = jnp.where(same_expert & same_slot, 1.0, 0.0).astype(jnp.float32)
    dispatch = jnp.sum(match, axis=3)
    combine = jnp.transpose(jnp.sum(match * weights[None, None, :, :], axis=3), (2, 0, 1))
    return (dispatch, combine)


def shards(
    queries,
    keys,
    values,
    residual,
    norm_gain,
    out_weight,
    gate_weight,
    up_weight,
    down_weight,
    expert_ids,
    route_weights,
):
    n_tp = lax.axis_size("tp")
    n_ep = lax.axis_size("ep")
    n_etp = lax.axis_size("etp")
    rows = queries.shape[0]
    heads_dev = queries.shape[1] // HD
    kv_dev = keys.shape[1] // HD
    group = heads_dev // kv_dev
    query_pos = lax.axis_index(("ep", "etp")) * rows + jnp.arange(rows, dtype=jnp.int32)
    grouped = queries.reshape(rows, kv_dev, group, HD)
    key_piece = lax.all_gather(keys, ("ep", "etp"), axis=0, tiled=True)
    value_piece = lax.all_gather(values, ("ep", "etp"), axis=0, tiled=True)
    count = key_piece.shape[0]
    key_heads = key_piece.reshape(count, kv_dev, HD)
    value_heads = value_piece.reshape(count, kv_dev, HD)
    scores = jnp.einsum(
        "qkgd,skd->qkgs", grouped, key_heads, preferred_element_type=jnp.float32
    ) / math.sqrt(HD)
    key_pos = jnp.arange(count, dtype=jnp.int32)
    visible = (key_pos[None, :] <= query_pos[:, None])[:, None, None, :]
    scores = jnp.where(visible, scores, -1e30)
    running = jnp.full((rows, kv_dev, group), -1e30, jnp.float32)
    newest = jnp.maximum(running, jnp.max(scores, axis=-1))
    probs = jnp.where(visible, jnp.exp(scores - newest[..., None]), 0.0)
    total = jnp.sum(probs, axis=-1)
    weighted = jnp.einsum(
        "qkgs,skd->qkgd",
        probs.astype(jnp.bfloat16),
        value_heads,
        preferred_element_type=jnp.float32,
    )
    running, total, accum = (newest, total, weighted)
    attention = (accum / total[..., None]).astype(jnp.bfloat16).reshape(rows, heads_dev * HD)
    moe_rows = rows // n_tp
    stacked = attention.reshape(n_tp, moe_rows, heads_dev * HD)
    partial_proj = jnp.einsum(
        "tmf,fc->tmc",
        lax.all_gather(stacked, "etp", axis=1, tiled=True),
        out_weight,
        preferred_element_type=jnp.float32,
    )
    cols = out_weight.shape[1]
    parts = lax.all_to_all(
        partial_proj.reshape(n_tp * n_etp, moe_rows, cols).astype(jnp.bfloat16),
        ("tp", "etp"),
        split_axis=0,
        concat_axis=0,
        tiled=True,
    ).astype(jnp.float32)
    projected = jnp.sum(parts.reshape(n_tp, n_etp, moe_rows, cols), axis=0)
    projected = jnp.transpose(projected, (1, 0, 2)).reshape(moe_rows, n_etp * cols)
    model = n_etp * cols
    state = residual.reshape(moe_rows, model).astype(jnp.float32) + projected
    scale_rows = lax.rsqrt(jnp.mean(state * state, axis=-1, keepdims=True) + 1e-05)
    normed = (state * scale_rows * norm_gain).astype(jnp.bfloat16)
    experts = n_ep * gate_weight.shape[0]
    top = expert_ids.shape[-1]
    cap = max(2, min(moe_rows, 5 * moe_rows * top // (4 * experts)))
    dispatch, combine = route_tables(
        expert_ids.reshape(moe_rows, top), route_weights.reshape(moe_rows, top), experts, cap
    )
    send = jnp.einsum(
        "ecm,md->ecd", dispatch.astype(jnp.bfloat16), normed, preferred_element_type=jnp.float32
    ).astype(jnp.bfloat16)
    gate_local = gate_weight[0]
    up_local = up_weight[0]
    down_local = down_weight[0]
    spread_out = jnp.broadcast_to(send[None, :, None], (n_tp, experts, n_etp, cap, model))
    arrived = lax.all_to_all(
        spread_out.reshape(n_tp * experts * n_etp, cap, model),
        ("tp", "ep", "etp"),
        split_axis=0,
        concat_axis=0,
        tiled=True,
    )
    piece = arrived.reshape(-1, model)
    gate_v = jnp.dot(piece, gate_local, preferred_element_type=jnp.float32)
    up_v = jnp.dot(piece, up_local, preferred_element_type=jnp.float32)
    inner = (jax.nn.silu(gate_v) * up_v).astype(jnp.bfloat16)
    terms = jnp.dot(inner, down_local, preferred_element_type=jnp.float32).astype(jnp.bfloat16)
    returned = lax.all_to_all(
        terms.reshape(-1, cap, model), ("tp", "ep", "etp"), split_axis=0, concat_axis=0, tiled=True
    )
    expert_out = jnp.sum(
        returned.reshape(n_tp, experts, n_etp, cap, model), axis=(0, 2), dtype=jnp.float32
    )
    moe = jnp.einsum("mec,ecd->md", combine, expert_out)
    mixed = (state + moe).astype(jnp.bfloat16).reshape(1, 1, moe_rows, model)
    return (attention, mixed)


def solution(mesh):
    return jax.shard_map(
        shards,
        mesh=mesh,
        in_specs=(
            P(("ep", "etp"), "tp"),
            P(("ep", "etp"), "tp"),
            P(("ep", "etp"), "tp"),
            P(("ep", "etp"), "tp", None, None),
            P(),
            P("tp", "etp"),
            P("ep", None, ("tp", "etp")),
            P("ep", None, ("tp", "etp")),
            P("ep", ("tp", "etp"), None),
            P(("ep", "etp"), "tp", None, None),
            P(("ep", "etp"), "tp", None, None),
        ),
        out_specs=(P(("ep", "etp"), "tp"), P(("ep", "etp"), "tp", None, None)),
        check_vma=False,
    )
```

profile of v0, /device:TPU:2, one launch (start us, length us, event | category | flops | bytes accessed | tf_op | source)
XLA Modules:
  0.0 970.7 jit_solution(11778429673031174929)
XLA Ops:
  7.2 0.0 all-gather.4.cloned.1.call-start
  7.2 1.6 copy.45
  8.8 0.0 all-gather.4.cloned.1.call-update
  8.8 0.0 all-gather.6.cloned.1.call-start
  8.9 0.7 all-gather.6.cloned.1.call-update
  9.6 0.0 all-gather.8.cloned.1.call-start
  9.6 1.9 copy.46
  11.5 0.3 iota_compare_fusion
  11.9 45.8 %all-gather.4.cloned.1.call-done = bf16[4096,256]{0,1:T(8,128)(2,1)} async-done(((bf16[128,256]{0,1:T(8,128)(2,1)}), bf16[4096,256]{0,1:T(8,128)(2,1)}) %all-gather.4.cloned.1.call-update) | async-done | bytes 2097168 | tf_op jit(solution)/shard_map/all_gather | solution.py:47
  57.7 5.4 fusion
  63.2 8.4 copy-done
  71.5 6.2 fusion.1
  77.8 25.5 %all-gather.6.cloned.1.call-done = bf16[4096,256]{1,0:T(8,128)(2,1)} async-done(((bf16[128,256]{1,0:T(8,128)(2,1)}), bf16[4096,256]{1,0:T(8,128)(2,1)}) %all-gather.6.cloned.1.call-update) | async-done | bytes 2097168 | tf_op jit(solution)/shard_map/all_gather | solution.py:48
  103.3 2.9 copy.49
  106.2 11.4 %fusion.32 = bf16[128,2,6,128]{0,3,2,1:T(8,128)(2,1)S(1)} fusion(bf16[4096,2,128,1]{0,2,3,1:T(8,128)(2,1)S(1)} %bitcast.109, f32[2,4096,128,6]{2,1,3,0:T(8,128)} %copy-done, f32[128,2,6]{0,2,1:T(8,128)S(1)} %broadcast_maximum_fusion, pred[128,4096]{0,1:T(8,128)(4,1)S(1)} %iota_compare_fusion, f32[128,2,6]{0,2,1:T(8,128)S(1)} %fusion.1), kind=kOutput, calls=%fused_computation.29 | convolution fusion | flops 1642463232 | bytes 28192768 | tf_op jit(solution)/shard_map/qkgs,skd->qkgd/dot_general | solution.py:62
  117.6 0.0 copy-start.3
  117.6 0.4 copy.51
  118.0 1.2 reshape_reshape.3
  119.2 0.0 all-gather.8.cloned.1.call-update
  119.3 0.0 copy-start.7
  119.3 26.4 %all-gather.8.cloned.1.call-done = bf16[4,128,1536]{2,1,0:T(8,128)(2,1)} async-done(((bf16[4,32,1536]{2,1,0:T(8,128)(2,1)}), bf16[4,128,1536]{2,1,0:T(8,128)(2,1)}) %all-gather.8.cloned.1.call-update) | async-done | bytes 1572880 | tf_op jit(solution)/shard_map/all_gather | solution.py:74
  145.7 6.6 fusion.19
  152.3 5.8 all-to-all-start
  158.1 0.1 copy.53
  158.2 0.1 eq.59
  158.3 0.1 fusion.45
  158.3 0.1 reduce_window_sum.11
  158.4 0.2 select_reduce_fusion.1
  158.6 0.1 eq.63
  158.7 0.1 copy.54
  158.8 0.6 reshape.113
  159.5 21.8 %all-to-all-done = bf16[16,32,1536]{2,1,0:T(8,128)(2,1)S(1)} async-done(((bf16[16,32,1536]{2,1,0:T(8,128)(2,1)}), bf16[16,32,1536]{2,1,0:T(8,128)(2,1)S(1)}, u32[]{:S(2)}, u32[]{:S(2)}) %all-to-all-start) | async-done | bytes 1572896 | tf_op jit(solution)/shard_map/all_to_all | solution.py:79
  181.4 0.2 convert_reduce_fusion.1
  181.6 0.4 fusion.36
  182.0 0.1 copy.67
  182.1 0.6 convolution_convert_fusion.1
  182.7 3.1 broadcast_in_dim.51
  185.9 286.3 %all_to_all.15 = bf16[128,10,6144]{2,1,0:T(8,128)(2,1)} all-to-all(bf16[128,10,6144]{2,1,0:T(8,128)(2,1)S(1)} %bitcast.103), channel_id=1, replica_groups=mesh['tp'=4,'ep'=8,'etp'=4] {'tp','ep','etp'}, dimensions={0} | all-to-all | bytes 31457280 | tf_op jit(solution)/shard_map/all_to_all | solution.py:105
  472.2 26.4 %reshape.107 = bf16[1280,6144]{1,0:T(8,128)(2,1)} reshape(bf16[128,10,6144]{2,1,0:T(8,128)(2,1)} %all_to_all.15) | data formatting | bytes 31457280 | tf_op jit(solution)/shard_map/reshape | solution.py:112
  498.6 14.7 %fusion.12 = f32[1280,512]{1,0:T(8,128)} fusion(bf16[1280,6144]{1,0:T(8,128)(2,1)} %reshape.107, bf16[1,6144,512]{2,1,0:T(8,128)(2,1)} %param.17), kind=kOutput, calls=%fused_computation.17 | convolution fusion | flops 8053063680 | bytes 24641536 | tf_op jit(solution)/shard_map/dot_general | solution.py:113
  513.3 12.2 %fusion.22 = bf16[1280,512]{1,0:T(8,128)(2,1)} fusion(bf16[1280,6144]{1,0:T(8,128)(2,1)S(1)} %copy-done.1, bf16[1,6144,512]{2,1,0:T(8,128)(2,1)} %param.18, f32[1280,512]{1,0:T(8,128)} %fusion.12), kind=kOutput, calls=%fused_computation.24 | convolution fusion | flops 8056995840 | bytes 25952256 | tf_op jit(solution)/shard_map/dot_general | solution.py:114
  525.5 12.5 %convolution_convert_fusion = bf16[1280,6144]{1,0:T(8,128)(2,1)} fusion(bf16[1280,512]{1,0:T(8,128)(2,1)} %fusion.22, bf16[1,512,6144]{2,1,0:T(8,128)(2,1)S(1)} %bitcast.115), kind=kOutput, calls=%fused_computation.3 | convolution fusion | flops 8060928000 | bytes 23330816 | tf_op jit(solution)/shard_map/dot_general | solution.py:116
  538.0 25.9 %reshape.108 = bf16[128,10,6144]{2,1,0:T(8,128)(2,1)} reshape(bf16[1280,6144]{1,0:T(8,128)(2,1)} %convolution_convert_fusion) | data formatting | bytes 31457280 | tf_op jit(solution)/shard_map/reshape | solution.py:118
  563.9 8.7 all-to-all-start.2
  572.6 0.9 copy.58
  573.6 375.4 %all-to-all-done.2 = bf16[128,10,6144]{2,1,0:T(8,128)(2,1)} async-done(((bf16[128,10,6144]{2,1,0:T(8,128)(2,1)}), bf16[128,10,6144]{2,1,0:T(8,128)(2,1)}, u32[]{:S(2)}, u32[]{:S(2)}) %all-to-all-start.2) | async-done | bytes 15728672 | tf_op jit(solution)/shard_map/all_to_all | solution.py:117
  948.9 13.7 %convert_reduce_fusion = bf16[8,10,6144]{2,1,0:T(8,128)(2,1)S(1)} fusion(bf16[4,8,4,10,6144]{4,3,2,1,0:T(8,128)(2,1)} %bitcast.30), kind=kLoop, calls=%fused_computation | loop fusion | flops 15237120 | bytes 16711680 | tf_op jit(solution)/shard_map/reduce_sum | solution.py:120
  962.7 1.5 fusion.8
  (24 shorter events, 0.1 us)
Async XLA Ops:
  7.2 50.6 %all-gather.4.cloned.1.call-start = ((), (), s32[]{:S(2)}) async-start(), calls=%async_computation.3 | async-start | bytes 2162688 | tf_op jit(solution)/shard_map/all_gather | solution.py:47
  8.8 94.5 %all-gather.6.cloned.1.call-start = ((), (), s32[]{:S(2)}) async-start(), calls=%async_computation.4 | async-start | bytes 2162688 | tf_op jit(solution)/shard_map/all_gather | solution.py:48
  9.6 136.2 %all-gather.8.cloned.1.call-start = ((), (), s32[]{:S(2)}) async-start(), calls=%async_computation.5 | async-start | bytes 1966080 | tf_op jit(solution)/shard_map/all_gather | solution.py:74
  63.2 8.4 copy-start
  117.6 34.7 %copy-start.3 = (bf16[128,2,6,128]{0,3,2,1:T(8,128)(2,1)}, bf16[128,2,6,128]{0,3,2,1:T(8,128)(2,1)S(1)}, u32[]{:S(2)}) copy-start(bf16[128,2,6,128]{0,3,2,1:T(8,128)(2,1)S(1)} %fusion.32) | copy-start | bytes 1179652
  119.2 38.8 %copy-start.6 = (s32[1,1,32,2]{2,3,1,0:T(2,128)S(1)}, s32[1,1,32,2]{2,3,1,0:T(2,128)}, u32[]{:S(2)}) copy-start(s32[1,1,32,2]{2,3,1,0:T(2,128)} %param.20) | copy-start | bytes 772
  119.3 39.6 %copy-start.2 = (bf16[1,1,32,6144]{3,2,1,0:T(8,128)(2,1)S(1)}, bf16[1,1,32,6144]{3,2,1,0:T(8,128)(2,1)}, u32[]{:S(2)}) copy-start(bf16[1,1,32,6144]{3,2,1,0:T(8,128)(2,1)} %param.14) | copy-start | bytes 1179652
  119.3 40.2 %copy-start.7 = (f32[1,1,32,2]{2,3,1,0:T(2,128)S(1)}, f32[1,1,32,2]{2,3,1,0:T(2,128)}, u32[]{:S(2)}) copy-start(f32[1,1,32,2]{2,3,1,0:T(2,128)} %param.21) | copy-start | bytes 772
  152.3 29.8 %copy-start.5 = (f32[6144]{0:T(1024)S(1)}, f32[6144]{0:T(1024)}, u32[]{:S(2)}) copy-start(f32[6144]{0:T(1024)} %param.15) | copy-start | bytes 73732
  152.3 29.1 %all-to-all-start = ((bf16[16,32,1536]{2,1,0:T(8,128)(2,1)}), bf16[16,32,1536]{2,1,0:T(8,128)(2,1)S(1)}, u32[]{:S(2)}, u32[]{:S(2)}) async-start(bf16[16,32,1536]{2,1,0:T(8,128)(2,1)} %bitcast.11), calls=%async_computation | async-start | bytes 3145728 | tf_op jit(solution)/shard_map/all_to_all | solution.py:79
  498.6 14.7 %copy-start.1 = (bf16[1280,6144]{1,0:T(8,128)(2,1)S(1)}, bf16[1280,6144]{1,0:T(8,128)(2,1)}, u32[]{:S(2)}) copy-start(bf16[1280,6144]{1,0:T(8,128)(2,1)} %reshape.107) | copy-start | bytes 47185924
  498.6 26.9 %slice-start = ((s8[6291456]{0:T(1024)(128)(4,1)}), s8[4194304]{0:T(1024)(128)(4,1)S(1)}, s32[]{:S(2)}) async-start(s8[6291456]{0:T(1024)(128)(4,1)} %bitcast.114), calls=%async_computation.6 | async-start | bytes 8388608
  513.3 12.2 %slice-start.1 = ((s8[6291456]{0:T(1024)(128)(4,1)}), s8[2097152]{0:T(1024)(128)(4,1)S(1)}, s32[]{:S(2)}) async-start(s8[6291456]{0:T(1024)(128)(4,1)} %bitcast.114), calls=%async_computation.7 | async-start | bytes 4194304
  563.9 8.8 copy-start.4
  563.9 385.1 %all-to-all-start.2 = ((bf16[128,10,6144]{2,1,0:T(8,128)(2,1)}), bf16[128,10,6144]{2,1,0:T(8,128)(2,1)}, u32[]{:S(2)}, u32[]{:S(2)}) async-start(bf16[128,10,6144]{2,1,0:T(8,128)(2,1)} %reshape.108), calls=%async_computation.2 | async-start | bytes 50331648 | tf_op jit(solution)/shard_map/all_to_all | solution.py:117
Sparse Core Ops, SparseCore 0:
  10.8 46.9 all-gather.3
  60.0 43.2 all-gather.5
  119.4 26.2 all-gather.7
where the time goes:
time: 973 us; the launch traced here: 971 us
  waiting for transfers between devices  496 us (51%)
  blocking collectives  286 us (29%)
  local copies, waits for them, and re-layouts  73.8 us (8%)
  matrix products  64.9 us (7%)
  other arithmetic  21.4 us (2%)
  starting transfers between devices  14.6 us (2%)
  between operations  14 us (1%)
    all_to_all x1, waiting for transfers between devices, shards(): lax.all_to_all(terms.reshape(-1, cap, model), ('tp', 'ep', 'etp'), split_...  375 us
    all_to_all x1, blocking collectives, shards(): lax.all_to_all(spread_out.reshape(n_tp * experts * n_etp, cap, model), ('...  286 us
    all_gather x1, waiting for transfers between devices, shards(): key_piece = lax.all_gather(keys, ('ep', 'etp'), axis=0, tiled=True)  45.8 us
    all_gather x1, waiting for transfers between devices, shards(): lax.all_gather(stacked, 'etp', axis=1, tiled=True)  26.4 us
    reshape x1, local copies, waits for them, and re-layouts, shards(): piece = arrived.reshape(-1, model)  26.4 us
    reshape x1, local copies, waits for them, and re-layouts, shards(): terms.reshape(-1, cap, model)  25.9 us
    all_gather x1, waiting for transfers between devices, shards(): value_piece = lax.all_gather(values, ('ep', 'etp'), axis=0, tiled=True)  25.5 us
    all_to_all x1, waiting for transfers between devices, shards(): lax.all_to_all(partial_proj.reshape(n_tp * n_etp, moe_rows, cols).astype(...  21.8 us
  transfers between devices with their start and end apart: 5, of which 5 were waited for; matrix products, arithmetic and copies ran while one was open for 2% of the time, Pallas kernels for 0%

commit v1 on v0

v1 whole, which is shorter than its diff:
```python
import math

import jax
import jax.numpy as jnp
from jax import lax
from jax.sharding import PartitionSpec as P

HD = 128


def route_slots(ids, experts):
    tokens, top = ids.shape
    flat = ids.reshape(-1)
    hot = (flat[:, None] == jnp.arange(experts, dtype=jnp.int32)[None, :]).astype(jnp.int32)
    rank = jnp.cumsum(hot, axis=0) - hot
    return jnp.sum(rank * hot, axis=1).reshape(tokens, top)


def split_bf16(x):
    hi = x.astype(jnp.bfloat16)
    lo = (x - hi.astype(jnp.float32)).astype(jnp.bfloat16)
    return hi, lo


def shards(
    queries,
    keys,
    values,
    residual,
    norm_gain,
    out_weight,
    gate_weight,
    up_weight,
    down_weight,
    expert_ids,
    route_weights,
):
    n_tp = lax.axis_size("tp")
    n_ep = lax.axis_size("ep")
    n_etp = lax.axis_size("etp")
    rows = queries.shape[0]
    heads_dev = queries.shape[1] // HD
    kv_dev = keys.shape[1] // HD
    group = heads_dev // kv_dev
    query_pos = lax.axis_index(("ep", "etp")) * rows + jnp.arange(rows, dtype=jnp.int32)
    grouped = queries.reshape(rows, kv_dev, group, HD)
    kv = lax.all_gather(
        jnp.concatenate([keys, values], axis=1), ("ep", "etp"), axis=0, tiled=True
    )
    count = kv.shape[0]
    key_heads = kv[:, : kv_dev * HD].reshape(count, kv_dev, HD)
    value_heads = kv[:, kv_dev * HD :].reshape(count, kv_dev, HD)
    scores = jnp.einsum(
        "qkgd,skd->qkgs", grouped, key_heads, preferred_element_type=jnp.float32
    ) / math.sqrt(HD)
    key_pos = jnp.arange(count, dtype=jnp.int32)
    visible = (key_pos[None, :] <= query_pos[:, None])[:, None, None, :]
    scores = jnp.where(visible, scores, -1e30)
    newest = jnp.max(scores, axis=-1)
    probs = jnp.where(visible, jnp.exp(scores - newest[..., None]), 0.0)
    total = jnp.sum(probs, axis=-1)
    weighted = jnp.einsum(
        "qkgs,skd->qkgd",
        probs.astype(jnp.bfloat16),
        value_heads,
        preferred_element_type=jnp.float32,
    )
    attention = (weighted / total[..., None]).astype(jnp.bfloat16).reshape(rows, heads_dev * HD)
    moe_rows = rows // n_tp
    stacked = attention.reshape(n_tp, moe_rows, heads_dev * HD)
    partial_proj = jnp.einsum(
        "tmf,fc->tmc",
        lax.all_gather(stacked, "etp", axis=1, tiled=True),
        out_weight,
        preferred_element_type=jnp.float32,
    )
    cols = out_weight.shape[1]
    parts = lax.all_to_all(
        partial_proj.reshape(n_tp * n_etp, moe_rows, cols).astype(jnp.bfloat16),
        ("tp", "etp"),
        split_axis=0,
        concat_axis=0,
        tiled=True,
    ).astype(jnp.float32)
    projected = jnp.sum(parts.reshape(n_tp, n_etp, moe_rows, cols), axis=0)
    projected = jnp.transpose(projected, (1, 0, 2)).reshape(moe_rows, n_etp * cols)
    model = n_etp * cols
    state = residual.reshape(moe_rows, model).astype(jnp.float32) + projected
    scale_rows = lax.rsqrt(jnp.mean(state * state, axis=-1, keepdims=True) + 1e-05)
    normed = (state * scale_rows * norm_gain).astype(jnp.bfloat16)
    experts = n_ep * gate_weight.shape[0]
    top = expert_ids.shape[-1]
    cap = max(2, min(moe_rows, 5 * moe_rows * top // (4 * experts)))
    ids = expert_ids.reshape(moe_rows, top)
    weights = route_weights.reshape(moe_rows, top)
    place = ids * cap + route_slots(ids, experts)
    match = place[:, :, None] == jnp.arange(experts * cap, dtype=jnp.int32)[None, None, :]
    dispatch = jnp.sum(match.astype(jnp.float32), axis=1)
    combine = jnp.sum(jnp.where(match, weights[:, :, None], 0.0), axis=1)
    send = lax.dot_general(
        dispatch.astype(jnp.bfloat16),
        normed,
        (((0,), (0,)), ((), ())),
        preferred_element_type=jnp.float32,
    ).astype(jnp.bfloat16)
    gate_local = gate_weight[0]
    up_local = up_weight[0]
    down_local = down_weight[0]
    own = lax.all_to_all(send, "ep", split_axis=0, concat_axis=0, tiled=True)
    piece = lax.all_gather(own, ("tp", "etp"), axis=0, tiled=True)
    gate_v = jnp.dot(piece, gate_local, preferred_element_type=jnp.float32)
    up_v = jnp.dot(piece, up_local, preferred_element_type=jnp.float32)
    inner = (jax.nn.silu(gate_v) * up_v).astype(jnp.bfloat16)
    terms = jnp.dot(inner, down_local, preferred_element_type=jnp.float32).astype(jnp.bfloat16)
    summed = lax.psum_scatter(terms, ("tp", "etp"), scatter_dimension=0, tiled=True)
    expert_out = lax.all_to_all(summed, "ep", split_axis=0, concat_axis=0, tiled=True)
    hi, lo = split_bf16(combine)
    moe = jnp.dot(hi, expert_out, preferred_element_type=jnp.float32) + jnp.dot(
        lo, expert_out, preferred_element_type=jnp.float32
    )
    mixed = (state + moe).astype(jnp.bfloat16).reshape(1, 1, moe_rows, model)
    return (attention, mixed)


def solution(mesh):
    return jax.shard_map(
        shards,
        mesh=mesh,
        in_specs=(
            P(("ep", "etp"), "tp"),
            P(("ep", "etp"), "tp"),
            P(("ep", "etp"), "tp"),
            P(("ep", "etp"), "tp", None, None),
            P(),
            P("tp", "etp"),
            P("ep", None, ("tp", "etp")),
            P("ep", None, ("tp", "etp")),
            P("ep", ("tp", "etp"), None),
            P(("ep", "etp"), "tp", None, None),
            P(("ep", "etp"), "tp", None, None),
        ),
        out_specs=(P(("ep", "etp"), "tp"), P(("ep", "etp"), "tp", None, None)),
        check_vma=False,
    )
```

time: 973 us -> 466 us (0.48)
  the two profiles are of different devices: /device:TPU:2 before, /device:TPU:1 now
where the time goes in v1:
time: 466 us; the launch traced here: 465 us
  waiting for transfers between devices  324 us (70%)
  matrix products  68.7 us (15%)
  blocking collectives  29.1 us (6%)
  local copies, waits for them, and re-layouts  16.3 us (3%)
  between operations  14 us (3%)
  starting transfers between devices  10.7 us (2%)
    reduce_scatter x1, waiting for transfers between devices, shards(): lax.psum_scatter(terms, ('tp', 'etp'), scatter_dimension=0, tiled=True)  105 us
    all_gather x1, waiting for transfers between devices, shards(): piece = lax.all_gather(own, ('tp', 'etp'), axis=0, tiled=True)  102 us
    all_gather x1, waiting for transfers between devices, shards(): lax.all_gather(jnp.concatenate([keys, values], axis=1), ('ep', 'etp'), ax...  52.3 us
    all_to_all x1, blocking collectives, shards(): own = lax.all_to_all(send, 'ep', split_axis=0, concat_axis=0, tiled=True)  29.1 us
    all_gather x1, waiting for transfers between devices, shards(): lax.all_gather(stacked, 'etp', axis=1, tiled=True)  25.9 us
    all_to_all x1, waiting for transfers between devices, shards(): lax.all_to_all(summed, 'ep', split_axis=0, concat_axis=0, tiled=True)  19.8 us
    all_to_all x1, waiting for transfers between devices, shards(): lax.all_to_all(partial_proj.reshape(n_tp * n_etp, moe_rows, cols).astype(...  18.8 us
    sub x1, matrix products, shards(): probs = jnp.where(visible, jnp.exp(scores - newest[..., None]), 0.0)  15.8 us
  transfers between devices with their start and end apart: 6, of which 6 were waited for; matrix products, arithmetic and copies ran while one was open for 1% of the time, Pallas kernels for 0%

profile of v1, /device:TPU:1, one launch (start us, length us, event | category | flops | bytes accessed | tf_op | source)
XLA Modules:
  0.0 465.2 jit_solution(7325891598126734593)
XLA Ops:
  7.2 0.0 all-gather.4.cloned.1.call-start
  7.2 0.9 copy.48
  8.2 1.0 copy.49
  9.1 0.7 pad_maximum_fusion
  9.8 0.0 all-gather.4.cloned.1.call-update
  9.8 0.0 all-gather.6.cloned.1.call-start
  9.9 1.2 copy.50
  11.1 0.3 iota_compare_fusion
  11.5 52.3 %all-gather.4.cloned.1.call-done = bf16[4096,512]{0,1:T(8,128)(2,1)} async-done(((bf16[128,512]{0,1:T(8,128)(2,1)}), bf16[4096,512]{0,1:T(8,128)(2,1)}) %all-gather.4.cloned.1.call-update) | async-done | bytes 4194320 | tf_op jit(solution)/shard_map/all_gather | solution.py:47
  63.8 3.9 fusion.49
  67.7 15.8 %fusion.50 = (f32[128,2,6]{0,2,1:T(8,128)S(1)}, bf16[128,2,6,4096]{0,3,2,1:T(8,128)(2,1)}) fusion(pred[128,4096]{0,1:T(8,128)(4,1)S(1)} %iota_compare_fusion, bf16[4096,2,128,1]{0,2,3,1:T(8,128)(2,1)} %bitcast.92, bf16[128,2,6,128]{0,3,2,1:T(8,128)(2,1)S(1)} %bitcast.94), kind=kOutput, calls=%fused_computation.57 | convolution fusion | flops 1648365568 | bytes 15603712 | tf_op jit(solution)/shard_map/sub | solution.py:60
  83.5 6.4 %fusion.34 = bf16[128,2,6,128]{0,3,2,1:T(8,128)(2,1)S(1)} fusion(bf16[4096,2,128,1]{0,2,3,1:T(8,128)(2,1)S(1)} %bitcast.91, bf16[128,2,6,4096]{0,3,2,1:T(8,128)(2,1)} %get-tuple-element.15, f32[128,2,6]{0,2,1:T(8,128)S(1)} %get-tuple-element.14), kind=kOutput, calls=%fused_computation.30 | convolution fusion | flops 1611005952 | bytes 15079424 | tf_op jit(solution)/shard_map/qkgs,skd->qkgd/dot_general | solution.py:62
  89.9 0.4 copy.54
  90.4 1.2 reshape_reshape.3
  91.6 25.9 %all-gather.6.cloned.1.call-done = bf16[4,128,1536]{2,1,0:T(8,128)(2,1)} async-done(((bf16[4,32,1536]{2,1,0:T(8,128)(2,1)}), bf16[4,128,1536]{2,1,0:T(8,128)(2,1)}) %all-gather.6.cloned.1.call-update) | async-done | bytes 1572880 | tf_op jit(solution)/shard_map/all_gather | solution.py:73
  117.5 6.6 %fusion.22 = bf16[4,128,1536]{2,1,0:T(8,128)(2,1)} fusion(bf16[4,128,1536]{2,1,0:T(8,128)(2,1)} %all-gather.6.cloned.1.call-done, bf16[1536,1536]{1,0:T(8,128)(2,1)} %param.16), kind=kOutput, calls=%fused_computation.25 | convolution fusion | flops 2416705536 | bytes 7864320 | tf_op jit(solution)/shard_map/tmf,fc->tmc/dot_general | solution.py:71
  124.1 5.0 %all-to-all-start = ((bf16[16,32,1536]{2,1,0:T(8,128)(2,1)}), bf16[16,32,1536]{2,1,0:T(8,128)(2,1)S(1)}, u32[]{:S(2)}, u32[]{:S(2)}) async-start(bf16[16,32,1536]{2,1,0:T(8,128)(2,1)} %bitcast.11), calls=%async_computation | async-start | bytes 3145728 | tf_op jit(solution)/shard_map/all_to_all | solution.py:78
  129.1 0.2 all-gather.8.cloned.1.call-start
  129.4 0.1 copy.56
  129.4 0.1 eq.28
  129.5 0.1 fusion.42
  129.6 0.1 reduce_window_sum.11
  129.7 0.2 select_reduce_fusion.1
  129.9 0.1 reshape.97
  130.0 0.1 copy.57
  130.1 0.6 reshape.102
  130.8 0.1 select_reduce_fusion
  130.9 18.8 %all-to-all-done = bf16[16,32,1536]{2,1,0:T(8,128)(2,1)S(1)} async-done(((bf16[16,32,1536]{2,1,0:T(8,128)(2,1)}), bf16[16,32,1536]{2,1,0:T(8,128)(2,1)S(1)}, u32[]{:S(2)}, u32[]{:S(2)}) %all-to-all-start) | async-done | bytes 1572896 | tf_op jit(solution)/shard_map/all_to_all | solution.py:78
  149.6 0.2 convert_reduce_fusion
  149.8 0.4 fusion.38
  150.3 0.1 copy.66
  150.3 0.5 convolution_convert_fusion.1
  150.8 0.4 all_to_all.20
  151.2 29.1 %all_to_all.29 = bf16[8,10,6144]{2,1,0:T(8,128)(2,1)} all-to-all(bf16[8,10,6144]{2,1,0:T(8,128)(2,1)S(1)} %all_to_all.20), channel_id=1, replica_groups=mesh['tp'=4,'ep'=8,'etp'=4] {'ep'}, dimensions={0} | all-to-all | bytes 1966080 | tf_op jit(solution)/shard_map/all_to_all | solution.py:109
  180.4 2.3 all_to_all.22
  182.8 0.0 reduce-scatter.2.cloned.1.call-start
  182.8 102.4 %all-gather.8.cloned.1.call-done = bf16[1280,6144]{1,0:T(8,128)(2,1)} async-done(((bf16[80,6144]{1,0:T(8,128)(2,1)}), bf16[1280,6144]{1,0:T(8,128)(2,1)}) %all-gather.8.cloned.1.call-update) | async-done | bytes 15728656 | tf_op jit(solution)/shard_map/all_gather | solution.py:110
  285.2 14.7 %fusion.13 = f32[1280,512]{1,0:T(8,128)} fusion(bf16[1280,6144]{1,0:T(8,128)(2,1)} %all-gather.8.cloned.1.call-done, bf16[1,6144,512]{2,1,0:T(8,128)(2,1)} %param.17), kind=kOutput, calls=%fused_computation.18 | convolution fusion | flops 8053063680 | bytes 24641536 | tf_op jit(solution)/shard_map/dot_general | solution.py:111
  299.9 11.4 %fusion.25 = bf16[1280,512]{1,0:T(8,128)(2,1)S(1)} fusion(bf16[1280,6144]{1,0:T(8,128)(2,1)S(1)} %copy-done.6, bf16[1,6144,512]{2,1,0:T(8,128)(2,1)} %param.18, f32[1280,512]{1,0:T(8,128)} %fusion.13), kind=kOutput, calls=%fused_computation.26 | convolution fusion | flops 8056995840 | bytes 25952256 | tf_op jit(solution)/shard_map/dot_general | solution.py:112
  311.4 11.1 %convolution_convert_fusion = bf16[1280,6144]{1,0:T(8,128)(2,1)} fusion(bf16[1280,512]{1,0:T(8,128)(2,1)S(1)} %fusion.25, bf16[1,512,6144]{2,1,0:T(8,128)(2,1)S(1)} %bitcast.97), kind=kOutput, calls=%fused_computation.3 | convolution fusion | flops 8060928000 | bytes 23330816 | tf_op jit(solution)/shard_map/dot_general | solution.py:114
  322.4 105.2 %reduce-scatter.2.cloned.1.call-done = bf16[80,6144]{1,0:T(8,128)(2,1)} async-done(((bf16[1280,6144]{1,0:T(8,128)(2,1)}), bf16[80,6144]{1,0:T(8,128)(2,1)}) %reduce-scatter.2.cloned.1.call-update) | async-done | bytes 983056 | tf_op jit(solution)/shard_map/reduce_scatter | solution.py:115
  427.6 2.4 all_to_all.23
  430.0 5.3 %all-to-all-start.2 = ((bf16[8,10,6144]{2,1,0:T(8,128)(2,1)}), bf16[8,10,6144]{2,1,0:T(8,128)(2,1)S(1)}, u32[]{:S(2)}, u32[]{:S(2)}) async-start(bf16[8,10,6144]{2,1,0:T(8,128)(2,1)} %all_to_all.23), calls=%async_computation.3 | async-start | bytes 3145728 | tf_op jit(solution)/shard_map/all_to_all | solution.py:116
  435.3 0.9 copy.59
  436.2 19.8 %all-to-all-done.2 = bf16[8,10,6144]{2,1,0:T(8,128)(2,1)S(1)} async-done(((bf16[8,10,6144]{2,1,0:T(8,128)(2,1)}), bf16[8,10,6144]{2,1,0:T(8,128)(2,1)S(1)}, u32[]{:S(2)}, u32[]{:S(2)}) %all-to-all-start.2) | async-done | bytes 983072 | tf_op jit(solution)/shard_map/all_to_all | solution.py:116
  456.0 0.4 all_to_all.25
  456.4 0.3 fusion.45
  456.7 2.0 fusion.9
  (25 shorter events, 0.1 us)
Async XLA Ops:
  7.2 56.6 %all-gather.4.cloned.1.call-start = ((), (), s32[]{:S(2)}) async-start(), calls=%async_computation.4 | async-start | bytes 4325376 | tf_op jit(solution)/shard_map/all_gather | solution.py:47
  9.8 107.7 %all-gather.6.cloned.1.call-start = ((), (), s32[]{:S(2)}) async-start(), calls=%async_computation.5 | async-start | bytes 1966080 | tf_op jit(solution)/shard_map/all_gather | solution.py:73
  89.9 34.2 %copy-start.1 = (bf16[128,2,6,128]{0,3,2,1:T(8,128)(2,1)}, bf16[128,2,6,128]{0,3,2,1:T(8,128)(2,1)S(1)}, u32[]{:S(2)}) copy-start(bf16[128,2,6,128]{0,3,2,1:T(8,128)(2,1)S(1)} %fusion.34) | copy-start | bytes 1179652
  91.6 37.8 %copy-start.4 = (s32[1,1,32,2]{2,3,1,0:T(2,128)S(1)}, s32[1,1,32,2]{2,3,1,0:T(2,128)}, u32[]{:S(2)}) copy-start(s32[1,1,32,2]{2,3,1,0:T(2,128)} %param.20) | copy-start | bytes 772
  91.6 38.5 %copy-start = (bf16[1,1,32,6144]{3,2,1,0:T(8,128)(2,1)S(1)}, bf16[1,1,32,6144]{3,2,1,0:T(8,128)(2,1)}, u32[]{:S(2)}) copy-start(bf16[1,1,32,6144]{3,2,1,0:T(8,128)(2,1)} %param.14) | copy-start | bytes 1179652
  124.1 6.7 %copy-start.5 = (f32[1,1,32,2]{2,3,1,0:T(2,128)S(1)}, f32[1,1,32,2]{2,3,1,0:T(2,128)}, u32[]{:S(2)}) copy-start(f32[1,1,32,2]{2,3,1,0:T(2,128)} %param.21) | copy-start | bytes 772
  124.1 25.5 %all-to-all-start = ((bf16[16,32,1536]{2,1,0:T(8,128)(2,1)}), bf16[16,32,1536]{2,1,0:T(8,128)(2,1)S(1)}, u32[]{:S(2)}, u32[]{:S(2)}) async-start(bf16[16,32,1536]{2,1,0:T(8,128)(2,1)} %bitcast.11), calls=%async_computation | async-start | bytes 3145728 | tf_op jit(solution)/shard_map/all_to_all | solution.py:78
  129.1 21.2 %copy-start.3 = (f32[6144]{0:T(1024)S(1)}, f32[6144]{0:T(1024)}, u32[]{:S(2)}) copy-start(f32[6144]{0:T(1024)} %param.15) | copy-start | bytes 73732
  129.1 156.1 %all-gather.8.cloned.1.call-start = ((), (), s32[]{:S(2)}) async-start(), calls=%async_computation.6 | async-start | bytes 16711680 | tf_op jit(solution)/shard_map/all_gather | solution.py:110
  182.8 244.8 %reduce-scatter.2.cloned.1.call-start = ((), (), s32[]{:S(2)}) async-start(), calls=%async_computation.7 | async-start | bytes 16711680 | tf_op jit(solution)/shard_map/reduce_scatter | solution.py:115
  285.2 14.7 %copy-start.6 = (bf16[1280,6144]{1,0:T(8,128)(2,1)S(1)}, bf16[1280,6144]{1,0:T(8,128)(2,1)}, u32[]{:S(2)}) copy-start(bf16[1280,6144]{1,0:T(8,128)(2,1)} %all-gather.8.cloned.1.call-done) | copy-start | bytes 47185924
  285.2 26.1 %slice-start = ((s8[6291456]{0:T(1024)(128)(4,1)}), s8[4194304]{0:T(1024)(128)(4,1)S(1)}, s32[]{:S(2)}) async-start(s8[6291456]{0:T(1024)(128)(4,1)} %bitcast.96), calls=%async_computation.8 | async-start | bytes 8388608
  299.9 11.4 %slice-start.1 = ((s8[6291456]{0:T(1024)(128)(4,1)}), s8[2097152]{0:T(1024)(128)(4,1)S(1)}, s32[]{:S(2)}) async-start(s8[6291456]{0:T(1024)(128)(4,1)} %bitcast.96), calls=%async_computation.9 | async-start | bytes 4194304
  322.4 112.9 %copy-start.2 = (bf16[128,2,6,128]{0,3,2,1:T(8,128)(2,1)S(1)}, bf16[128,2,6,128]{0,3,2,1:T(8,128)(2,1)}, u32[]{:S(2)}) copy-start(bf16[128,2,6,128]{0,3,2,1:T(8,128)(2,1)} %copy-done.1) | copy-start | bytes 1179652
  430.0 26.0 %all-to-all-start.2 = ((bf16[8,10,6144]{2,1,0:T(8,128)(2,1)}), bf16[8,10,6144]{2,1,0:T(8,128)(2,1)S(1)}, u32[]{:S(2)}, u32[]{:S(2)}) async-start(bf16[8,10,6144]{2,1,0:T(8,128)(2,1)} %all_to_all.23), calls=%async_computation.3 | async-start | bytes 3145728 | tf_op jit(solution)/shard_map/all_to_all | solution.py:116
Sparse Core Ops, SparseCore 0:
  10.8 52.9 all-gather.3
  91.7 25.7 all-gather.5
  182.9 102.2 all-gather.7
  322.6 105.0 reduce-scatter.1
